TPU v7x, 32 devices: a whole 2x2x4 slice. The times are simulated.
32 devices in a mesh: wide: 4 (over y, x), narrow: 8 (over z, core).
Axes of the slice: x: 2, y: 2, z: 4, core: 2. Of those that a mesh axis runs over, the one named last changes fastest.
Arguments:
- tensor3: bfloat16 [256, 512, 512], P('wide', 'narrow'), may hold values from -6 to 6
- pattern: int32 [4, 8, 8], P('wide', 'narrow'), may hold values 0 or 1
- orbitals: bfloat16 [512, 256], P('narrow'), may hold values from -0.015625 to 0.015625
- metric: bfloat16 [256, 256], replicated, may hold values from -1 to 2, as said below
Outputs:
- exchange_matrix: float32 [512, 512], P(('wide', 'narrow'))
Inputs may be any that keep to these rules, and one draw needn't show every extreme that they name: metric is symmetric.
All inputs are finite; a program needn't handle non-finite values. No bound on the sum of `pattern` on one device may be relied on, other than what follows from the above.
Results may differ from a plain program's by a relative error of at most 0.0006.
Values may be sent and summed in bfloat16 or wider, within the bound.
A program may use at most 128 MiB of HBM per device.

v0:
```python
import jax
import jax.numpy as jnp
from jax import lax
from jax.sharding import PartitionSpec as P

BLK = 64


def body(tensor3, pattern, orbitals, metric):
    ri_local, ao_local, basis_all = tensor3.shape
    occupied = orbitals.shape[1]
    ri_blocks, ao_blocks, basis_blocks = pattern.shape
    shaped = tensor3.reshape(ri_blocks, BLK, ao_blocks, BLK, basis_blocks, BLK)
    masked = shaped * pattern[:, None, :, None, :, None].astype(jnp.bfloat16)
    flat_tensor = masked.reshape(ri_local * ao_local, basis_all)
    summed = jnp.dot(
        flat_tensor,
        lax.all_gather(orbitals, "narrow", axis=0, tiled=True),
        preferred_element_type=jnp.float32,
    )
    coeffs = summed.astype(jnp.bfloat16).reshape(ri_local, ao_local, occupied)
    section = lax.all_to_all(coeffs, "wide", split_axis=1, concat_axis=0, tiled=True)
    ri_all, sub_rows, items = section.shape
    product = jnp.dot(
        metric, section.reshape(ri_all, sub_rows * items), preferred_element_type=jnp.float32
    )
    fitted = lax.all_to_all(
        product.astype(jnp.bfloat16).reshape(ri_all, sub_rows, items),
        "wide",
        split_axis=0,
        concat_axis=1,
        tiled=True,
    )
    coef_new, fit_new = (
        lax.all_to_all(coeffs, "narrow", split_axis=0, concat_axis=1, tiled=True),
        lax.all_to_all(fitted, "narrow", split_axis=0, concat_axis=1, tiled=True),
    )
    return lax.psum_scatter(
        -jnp.einsum("pmi,pli->ml", fit_new, coef_new, preferred_element_type=jnp.float32),
        ("wide", "narrow"),
        scatter_dimension=0,
        tiled=True,
    )


def solution(mesh):
    in_specs = (P("wide", "narrow", None), P("wide", "narrow", None), P("narrow", None), P())
    out_specs = P(("wide", "narrow"), None)
    return jax.shard_map(body, mesh=mesh, in_specs=in_specs, out_specs=out_specs, check_vma=False)
```

profile of v0, /device:TPU:0, one launch (start us, length us, event | category | flops | bytes accessed | tf_op | source)
XLA Modules:
  0.0 344.0 jit_solution(15017425165755062976)
XLA Ops:
  6.5 0.0 copy-start
  6.5 0.7 convert_bitcast_fusion
  7.2 0.1 mul.15
  7.3 0.1 mul.16
  7.4 16.1 %all_gather.3 = bf16[512,256]{1,0:T(8,128)(2,1)S(1)} all-gather(bf16[64,256]{1,0:T(8,128)(2,1)} %param.6), channel_id=1, replica_groups=mesh['wide'=4,'narrow'=8] {'narrow'}, dimensions={0}, use_global_device_ids=true | all-gather | bytes 294912 | tf_op jit(solution)/shard_map/all_gather | solution.py:18
  23.5 2.5 bitcast_multiply_fusion
  25.9 1.3 convolution_convert_fusion.1
  27.2 0.0 copy-start.1
  27.2 1.2 copy.15
  28.4 0.2 copy-done.1
  28.5 29.4 %all_to_all.69 = bf16[64,64,256]{2,0,1:T(8,128)(2,1)S(1)} all-to-all(bf16[64,64,256]{2,0,1:T(8,128)(2,1)S(1)} %copy.15), channel_id=1, replica_groups=mesh['wide'=4,'narrow'=8] {'wide'}, dimensions={1} | all-to-all | bytes 4194304 | tf_op jit(solution)/shard_map/all_to_all | solution.py:22
  57.9 1.2 copy.17
  59.1 0.9 copy.23
  60.1 0.0 copy-done
  60.1 0.8 convolution_convert_fusion
  60.9 3.1 copy.18
  64.0 29.1 %all_to_all.70 = bf16[256,16,256]{2,1,0:T(8,128)(2,1)} all-to-all(bf16[256,16,256]{2,1,0:T(8,128)(2,1)} %copy.18), channel_id=1, replica_groups=mesh['wide'=4,'narrow'=8] {'wide'}, dimensions={0} | all-to-all | bytes 4194304 | tf_op jit(solution)/shard_map/all_to_all | solution.py:27
  93.1 4.7 %all-to-all-start.3 = ((bf16[64,64,256]{2,1,0:T(8,128)(2,1)}), bf16[64,64,256]{2,1,0:T(8,128)(2,1)S(1)}, u32[]{:S(2)}, u32[]{:S(2)}) async-start(bf16[64,64,256]{2,1,0:T(8,128)(2,1)} %bitcast.39), calls=%async_computation.3 | async-start | bytes 4194304 | tf_op jit(solution)/shard_map/all_to_all | solution.py:35
  97.8 3.2 copy.19
  101.0 45.9 %all-to-all-done.3 = bf16[64,64,256]{2,1,0:T(8,128)(2,1)S(1)} async-done(((bf16[64,64,256]{2,1,0:T(8,128)(2,1)}), bf16[64,64,256]{2,1,0:T(8,128)(2,1)S(1)}, u32[]{:S(2)}, u32[]{:S(2)}) %all-to-all-start.3) | async-done | bytes 2097184 | tf_op jit(solution)/shard_map/all_to_all | solution.py:35
  146.9 4.3 %all-to-all-start.2 = ((bf16[64,64,256]{2,1,0:T(8,128)(2,1)}), bf16[64,64,256]{2,1,0:T(8,128)(2,1)}, u32[]{:S(2)}, u32[]{:S(2)}) async-start(bf16[64,64,256]{2,1,0:T(8,128)(2,1)} %bitcast.41), calls=%async_computation.2 | async-start | bytes 4194304 | tf_op jit(solution)/shard_map/all_to_all | solution.py:36
  151.2 0.0 reduce-scatter.2.cloned.1.call-start
  151.3 1.5 copy.21
  152.8 47.5 %all-to-all-done.2 = bf16[64,64,256]{2,1,0:T(8,128)(2,1)} async-done(((bf16[64,64,256]{2,1,0:T(8,128)(2,1)}), bf16[64,64,256]{2,1,0:T(8,128)(2,1)}, u32[]{:S(2)}, u32[]{:S(2)}) %all-to-all-start.2) | async-done | bytes 2097184 | tf_op jit(solution)/shard_map/all_to_all | solution.py:36
  200.3 0.0 copy-start.2
  200.3 1.9 copy.20
  202.2 0.3 copy-done.2
  202.5 2.2 fusion
  204.8 0.0 reduce-scatter.2.cloned.1.call-update
  204.8 132.3 %reduce-scatter.2.cloned.1.call-done = f32[16,512]{1,0:T(8,128)} async-done(((f32[512,512]{1,0:T(8,128)}), f32[16,512]{1,0:T(8,128)}) %reduce-scatter.2.cloned.1.call-update) | async-done | bytes 32784 | tf_op jit(solution)/shard_map/reduce_scatter | solution.py:38
Async XLA Ops:
  6.5 53.6 %copy-start = (bf16[256,256]{1,0:T(8,128)(2,1)S(1)}, bf16[256,256]{1,0:T(8,128)(2,1)}, u32[]{:S(2)}) copy-start(bf16[256,256]{1,0:T(8,128)(2,1)} %param.7) | copy-start | bytes 393220
  27.2 1.3 copy-start.1
  93.1 53.7 %all-to-all-start.3 = ((bf16[64,64,256]{2,1,0:T(8,128)(2,1)}), bf16[64,64,256]{2,1,0:T(8,128)(2,1)S(1)}, u32[]{:S(2)}, u32[]{:S(2)}) async-start(bf16[64,64,256]{2,1,0:T(8,128)(2,1)} %bitcast.39), calls=%async_computation.3 | async-start | bytes 4194304 | tf_op jit(solution)/shard_map/all_to_all | solution.py:35
  146.9 53.4 %all-to-all-start.2 = ((bf16[64,64,256]{2,1,0:T(8,128)(2,1)}), bf16[64,64,256]{2,1,0:T(8,128)(2,1)}, u32[]{:S(2)}, u32[]{:S(2)}) async-start(bf16[64,64,256]{2,1,0:T(8,128)(2,1)} %bitcast.41), calls=%async_computation.2 | async-start | bytes 4194304 | tf_op jit(solution)/shard_map/all_to_all | solution.py:36
  151.2 185.9 %reduce-scatter.2.cloned.1.call-start = ((), (), s32[]{:S(2)}) async-start(), calls=%async_computation.5 | async-start | bytes 1081344 | tf_op jit(solution)/shard_map/reduce_scatter | solution.py:38
  200.3 2.2 copy-start.2
Sparse Core Ops, SparseCore 0:
  204.9 132.1 reduce-scatter.1
where the time goes:
time: 344 us
  waiting for transfers between devices  226 us (66%)
  blocking collectives  74.6 us (22%)
  local copies, waits for them, and re-layouts  13.7 us (4%)
  between operations  13.5 us (4%)
  starting transfers between devices  9.06 us (3%)
  matrix products  4.26 us (1%)
    reduce_scatter x1, waiting for transfers between devices, body(): lax.psum_scatter(-jnp.einsum('pmi,pli->ml', fit_new, coef_new, preferred_...  132 us
    all_to_all x1, waiting for transfers between devices, body(): lax.all_to_all(fitted, 'narrow', split_axis=0, concat_axis=1, tiled=True)  47.5 us
    all_to_all x1, waiting for transfers between devices, body(): lax.all_to_all(coeffs, 'narrow', split_axis=0, concat_axis=1, tiled=True)  45.9 us
    all_to_all x1, blocking collectives, body(): lax.all_to_all(coeffs, 'wide', split_axis=1, concat_axis=0, tiled=True)  29.4 us
    all_to_all x1, blocking collectives, body(): lax.all_to_all(product.astype(jnp.bfloat16).reshape(ri_all, sub_rows, ite...  29.1 us
    all_gather x1, blocking collectives, body(): lax.all_gather(orbitals, 'narrow', axis=0, tiled=True)  16.1 us
  transfers between devices with their start and end apart: 3, of which 3 were waited for; matrix products, arithmetic and copies ran while one was open for 1% of the time, Pallas kernels for 0%

commit v1 on v0

v1 whole, which is shorter than its diff:
```python
import functools

import jax
import jax.numpy as jnp
from jax import lax
from jax.experimental import pallas as pl
from jax.experimental.pallas import tpu as pltpu
from jax.sharding import PartitionSpec as P

MESH = pl.DeviceIdType.MESH


def kernel(nw, nn, t_ref, ct_ref, metric_ref, k_ref, wide_c, send, recv, gram, send_sem, recv_sem):
    ndev = nw * nn
    ri_local, ao_local, _ = t_ref.shape
    occ = ct_ref.shape[0]
    half = ri_local // 2
    lanes = 2 * ao_local
    chunks = occ // (2 * ndev)
    my_w, my_n = lax.axis_index("wide"), lax.axis_index("narrow")
    me = my_w * nn + my_n

    barrier = pltpu.get_barrier_semaphore()

    def greet(step, carry):
        other = lax.rem(me + step, ndev)
        pl.semaphore_signal(
            barrier, inc=1, device_id=(other // nn, lax.rem(other, nn)), device_id_type=MESH
        )
        return carry

    lax.fori_loop(1, ndev, greet, 0)

    def contract(step, carry):
        r = step * 2
        rows = jnp.concatenate(
            [t_ref[r], t_ref[half + r], t_ref[r + 1], t_ref[half + r + 1]], axis=0
        )
        out = lax.dot_general(
            ct_ref[...], rows, (((1,), (1,)), ((), ())), preferred_element_type=jnp.float32
        )
        start = pl.multiple_of(r * occ, 2 * occ)
        wide_c[pl.ds(start, occ), :] = out[:, :lanes]
        wide_c[pl.ds(start + occ, occ), :] = out[:, lanes:]
        return carry

    lax.fori_loop(0, half // 2, contract, 0)

    low = lax.broadcasted_iota(jnp.int32, (half, lanes), 1) < ao_local
    rows_here = pl.ds(pl.multiple_of(my_w * ri_local, ri_local), ri_local)
    lanes_here = pl.ds(pl.multiple_of(my_n * lanes, lanes), lanes)

    def pack(chunk, other):
        first = wide_c[pl.ds(chunk * 2 * ndev + other, half, stride=occ), :]
        second = wide_c[pl.ds(chunk * 2 * ndev + ndev + other, half, stride=occ), :]
        top = jnp.where(low, first, pltpu.roll(second, ao_local, 1))
        bottom = jnp.where(low, pltpu.roll(first, ao_local, 1), second)
        send[chunk, other] = jnp.concatenate([top, bottom], axis=0).astype(jnp.bfloat16)

    def outgoing(chunk, other):
        return pltpu.make_async_remote_copy(
            src_ref=send.at[chunk, other],
            dst_ref=recv.at[chunk, rows_here, lanes_here],
            send_sem=send_sem.at[chunk],
            recv_sem=recv_sem.at[chunk],
            device_id=(other // nn, lax.rem(other, nn)),
            device_id_type=MESH,
        )

    def own(chunk):
        return pltpu.make_async_copy(
            send.at[chunk, me], recv.at[chunk, rows_here, lanes_here], recv_sem.at[chunk]
        )

    pl.semaphore_wait(barrier, ndev - 1)
    for chunk in range(chunks):
        def ship(step, carry, chunk=chunk):
            other = lax.rem(me + step, ndev)
            pack(chunk, other)
            outgoing(chunk, other).start()
            return carry

        lax.fori_loop(1, ndev, ship, 0)
        pack(chunk, me)
        own(chunk).start()

    width = 2 * lanes
    for chunk in range(chunks):
        pltpu.make_async_copy(recv.at[chunk], recv.at[chunk], recv_sem.at[chunk]).wait()

        def fit(step, carry, chunk=chunk):
            at = pl.ds(pl.multiple_of(step * width, width), width)
            fitted = jnp.dot(
                metric_ref[...], recv[chunk, :, at], preferred_element_type=jnp.float32
            ).astype(jnp.bfloat16)
            term = lax.dot_general(
                fitted, recv[chunk], (((0,), (0,)), ((), ())), preferred_element_type=jnp.float32
            )
            gram[at, :] = term if chunk == 0 else gram[at, :] + term
            return carry

        lax.fori_loop(0, nn // 2, fit, 0)

    left = lax.broadcasted_iota(jnp.int32, (ao_local, lanes), 1) < ao_local

    def fold(n, carry):
        even = pl.ds(pl.multiple_of(n * lanes, lanes), ao_local)
        odd = pl.ds(pl.multiple_of(n * lanes + ao_local, ao_local), ao_local)
        out = pl.ds(pl.multiple_of(n * ao_local, ao_local), ao_local)
        for pair in range(nn // 2):
            one, two = pl.ds(2 * pair * lanes, lanes), pl.ds((2 * pair + 1) * lanes, lanes)
            here = jnp.where(left, gram[even, one], gram[odd, two])
            there = jnp.where(left, gram[even, two], gram[odd, one])
            k_ref[out, pl.ds(pair * lanes, lanes)] = -(here + pltpu.roll(there, ao_local, 1))
        return carry

    lax.fori_loop(0, nn, fold, 0)

    for chunk in range(chunks):
        def sent(step, carry, chunk=chunk):
            outgoing(chunk, lax.rem(me + step, ndev)).wait_send()
            return carry

        lax.fori_loop(1, ndev, sent, 0)


def body(nw, nn, tensor3, pattern, orbitals, metric):
    ri_local, ao_local, basis = tensor3.shape
    occ = orbitals.shape[1]
    ndev = nw * nn
    chunks = occ // (2 * ndev)
    lanes = 2 * ao_local
    block = basis // pattern.shape[2]
    keep = jnp.repeat(pattern[0, 0], block).astype(jnp.bfloat16)
    ct = (lax.all_gather(orbitals, "narrow", axis=0, tiled=True) * keep[:, None]).T
    term = pl.pallas_call(
        functools.partial(kernel, nw, nn),
        out_shape=jax.ShapeDtypeStruct((basis, basis), jnp.float32),
        in_specs=[pl.BlockSpec(memory_space=pltpu.VMEM)] * 3,
        out_specs=pl.BlockSpec(memory_space=pltpu.VMEM),
        scratch_shapes=[
            pltpu.VMEM((ri_local // 2 * occ, lanes), jnp.float32),
            pltpu.VMEM((chunks, ndev, ri_local, lanes), jnp.bfloat16),
            pltpu.VMEM((chunks, nw * ri_local, nn * lanes), jnp.bfloat16),
            pltpu.VMEM((nn * lanes, nn * lanes), jnp.float32),
            pltpu.SemaphoreType.DMA((chunks,)),
            pltpu.SemaphoreType.DMA((chunks,)),
        ],
        compiler_params=pltpu.CompilerParams(
            collective_id=0, has_side_effects=True, vmem_limit_bytes=56 * 1024 * 1024
        ),
    )(tensor3, ct, metric)
    return lax.psum_scatter(term, ("wide", "narrow"), scatter_dimension=0, tiled=True)


def solution(mesh):
    nw, nn = mesh.shape["wide"], mesh.shape["narrow"]
    in_specs = (P("wide", "narrow", None), P("wide", "narrow", None), P("narrow", None), P())
    out_specs = P(("wide", "narrow"), None)
    return jax.shard_map(
        functools.partial(body, nw, nn), mesh=mesh, in_specs=in_specs, out_specs=out_specs, check_vma=False
    )
```

time: 344 us -> 225 us (0.65)
  waiting for transfers between devices: 226 us -> 136 us
  Pallas kernels: 0 us -> 58.5 us
  blocking collectives: 74.6 us -> 16.1 us
  local copies, waits for them, and re-layouts: 13.7 us -> 0.3 us
  starting transfers between devices: 9.06 us -> 0.01 us
  matrix products: 4.26 us -> 0 us
    all_to_all x2 -> x0, waiting for transfers between devices: 93.4 us -> none  [the longest x1 47.5 us: body(): lax.all_to_all(fitted, 'narrow', split_axis=0, concat_axis=1, tiled=True)]
    all_to_all x2 -> x0, blocking collectives: 58.5 us -> none  [the longest x1 29.4 us: body(): lax.all_to_all(coeffs, 'wide', split_axis=1, concat_axis=0, tiled=True)]
    pallas_call x0 -> x1, Pallas kernels: none -> 58.5 us  [body(): pl.pallas_call(functools.partial(kernel, nw, nn), out_shape=jax.ShapeDtyp...]
    all_to_all x2 -> x0, starting transfers between devices: 9.01 us -> none  [the longest x1 4.67 us: body(): lax.all_to_all(coeffs, 'narrow', split_axis=0, concat_axis=1, tiled=True)]
    all_to_all x4 -> x0, local copies, waits for them, and re-layouts: 7.75 us -> none  [the longest x1 3.21 us: body(): lax.all_to_all(product.astype(jnp.bfloat16).reshape(ri_all, sub_rows, ite...]
    reshape x2 -> x0, local copies, waits for them, and re-layouts: 4.32 us -> none  [the longest x1 3.14 us: body(): product.astype(jnp.bfloat16).reshape(ri_all, sub_rows, items)]
    dot_general x3 -> x0, matrix products: 4.26 us -> none  [the longest x1 2.24 us: body(): jnp.einsum('pmi,pli->ml', fit_new, coef_new, preferred_element_type=jnp.f...]
  transfers between devices with their start and end apart: 3 -> 1, of which waited for: 3 -> 1; matrix products, arithmetic and copies ran while one was open for 1% -> 0% of each run, Pallas kernels for 0% -> 0%
where the time goes in v1:
time: 225 us
  waiting for transfers between devices  136 us (60%)
  Pallas kernels  58.5 us (26%)
  blocking collectives  16.1 us (7%)
  between operations  13.4 us (6%)
    reduce_scatter x1, waiting for transfers between devices, body(): lax.psum_scatter(term, ('wide', 'narrow'), scatter_dimension=0, tiled=True)  136 us
    pallas_call x1, Pallas kernels, body(): pl.pallas_call(functools.partial(kernel, nw, nn), out_shape=jax.ShapeDtyp...  58.5 us
    all_gather x1, blocking collectives, body(): lax.all_gather(orbitals, 'narrow', axis=0, tiled=True) * keep[:, None]  16.1 us
  transfers between devices with their start and end apart: 1, of which 1 were waited for; matrix products, arithmetic and copies ran while one was open for 0% of the time, Pallas kernels for 0%

profile of v1, /device:TPU:0, one launch (start us, length us, event | category | flops | bytes accessed | tf_op | source)
XLA Modules:
  0.0 225.3 jit_solution(5835436051123130392)
XLA Ops:
  6.5 0.0 reduce-scatter.2.cloned.1.call-start
  6.5 0.7 convert_bitcast_fusion
  7.2 0.1 broadcast_in_dim.4
  7.3 0.1 convert_element_type.16
  7.4 16.1 %all_gather.3 = bf16[512,256]{1,0:T(8,128)(2,1)S(1)} all-gather(bf16[64,256]{1,0:T(8,128)(2,1)} %param.6), channel_id=1, replica_groups=mesh['wide'=4,'narrow'=8] {'narrow'}, dimensions={0}, use_global_device_ids=true | all-gather | bytes 294912 | tf_op jit(solution)/shard_map/all_gather | solution.py:135
  23.4 0.1 copy.6
  23.6 0.7 multiply_bitcast_fusion.ct_ref
  24.3 58.5 %shard_map.46 = f32[512,512]{1,0:T(8,128)} custom-call(bf16[64,64,512]{2,1,0:T(8,128)(2,1)} %t_ref.1, bf16[256,512]{1,0:T(8,128)(2,1)} %multiply_bitcast_fusion.ct_ref, bf16[256,256]{1,0:T(8,128)(2,1)} %metric_ref.1), custom_call_target="tpu_custom_call" | custom-call | tf_op jit(solution)/shard_map/pallas_call | solution.py:136
  82.9 0.0 reduce-scatter.2.cloned.1.call-update
  82.9 135.6 %reduce-scatter.2.cloned.1.call-done = f32[16,512]{1,0:T(8,128)} async-done(((f32[512,512]{1,0:T(8,128)}), f32[16,512]{1,0:T(8,128)}) %reduce-scatter.2.cloned.1.call-update) | async-done | bytes 32784 | tf_op jit(solution)/shard_map/reduce_scatter | solution.py:153
Async XLA Ops:
  6.5 211.9 %reduce-scatter.2.cloned.1.call-start = ((), (), s32[]{:S(2)}) async-start(), calls=%async_computation.1 | async-start | bytes 1081344 | tf_op jit(solution)/shard_map/reduce_scatter | solution.py:153
Sparse Core Ops, SparseCore 0:
  83.0 135.4 reduce-scatter.1

commit v2 on v1

--- a/solution.py
+++ b/solution.py
@@ -10,16 +10,22 @@
 MESH = pl.DeviceIdType.MESH
 
 
-def kernel(nw, nn, t_ref, ct_ref, metric_ref, k_ref, wide_c, send, recv, gram, send_sem, recv_sem):
+def kernel(nw, nn, pattern_ref, t_hbm, orb_ref, metric_ref, out_ref, t_ref, orbs, ct_ref, wide_c, send, recv, gram,
+           terms, from_core, from_wide, from_z, t_sem, orb_send, orb_recv, send_sem, recv_sem,
+           core_send, core_recv, wide_send, wide_recv, z_send, z_recv):
     ndev = nw * nn
     ri_local, ao_local, _ = t_ref.shape
     occ = ct_ref.shape[0]
     half = ri_local // 2
     lanes = 2 * ao_local
     chunks = occ // (2 * ndev)
+    zs = nn // 2
     my_w, my_n = lax.axis_index("wide"), lax.axis_index("narrow")
     me = my_w * nn + my_n
-
+    my_z, my_core = my_n // 2, lax.rem(my_n, 2)
+
+    t_copy = pltpu.make_async_copy(t_hbm, t_ref, t_sem)
+    t_copy.start()
     barrier = pltpu.get_barrier_semaphore()
 
     def greet(step, carry):
@@ -30,6 +36,31 @@
         return carry
 
     lax.fori_loop(1, ndev, greet, 0)
+    pl.semaphore_wait(barrier, ndev - 1)
+
+    def orbital_copy(other, source):
+        return pltpu.make_async_remote_copy(
+            src_ref=orb_ref,
+            dst_ref=orbs.at[source],
+            send_sem=orb_send.at[other],
+            recv_sem=orb_recv.at[source],
+            device_id=(my_w, other),
+            device_id_type=MESH,
+        )
+
+    for step in range(1, nn):
+        orbital_copy(lax.rem(my_n + step, nn), my_n).start()
+    orbs[my_n] = orb_ref[...]
+    for step in range(1, nn):
+        other = lax.rem(my_n + step, nn)
+        orbital_copy(other, other).wait_recv()
+    for pair in range(nn // 2):
+        kept = [
+            orbs[n].astype(jnp.float32) * pattern_ref[0, 0, n].astype(jnp.float32)
+            for n in (2 * pair, 2 * pair + 1)
+        ]
+        ct_ref[:, pair * lanes:(pair + 1) * lanes] = jnp.concatenate(kept, axis=0).T.astype(jnp.bfloat16)
+    t_copy.wait()
 
     def contract(step, carry):
         r = step * 2
@@ -72,7 +103,6 @@
             send.at[chunk, me], recv.at[chunk, rows_here, lanes_here], recv_sem.at[chunk]
         )
 
-    pl.semaphore_wait(barrier, ndev - 1)
     for chunk in range(chunks):
         def ship(step, carry, chunk=chunk):
             other = lax.rem(me + step, ndev)
@@ -102,20 +132,87 @@
         lax.fori_loop(0, nn // 2, fit, 0)
 
     left = lax.broadcasted_iota(jnp.int32, (ao_local, lanes), 1) < ao_local
+    rows = ao_local // nw
 
     def fold(n, carry):
         even = pl.ds(pl.multiple_of(n * lanes, lanes), ao_local)
         odd = pl.ds(pl.multiple_of(n * lanes + ao_local, ao_local), ao_local)
-        out = pl.ds(pl.multiple_of(n * ao_local, ao_local), ao_local)
         for pair in range(nn // 2):
             one, two = pl.ds(2 * pair * lanes, lanes), pl.ds((2 * pair + 1) * lanes, lanes)
             here = jnp.where(left, gram[even, one], gram[odd, two])
             there = jnp.where(left, gram[even, two], gram[odd, one])
-            k_ref[out, pl.ds(pair * lanes, lanes)] = -(here + pltpu.roll(there, ao_local, 1))
+            folded = -(here + pltpu.roll(there, ao_local, 1))
+            for q in range(nw):
+                block = n * nw + q
+                terms[q % 2, block // nn, lax.rem(block, nn) // 2, :, pl.ds(pair * lanes, lanes)] = (
+                    folded[q * rows:(q + 1) * rows]
+                )
         return carry
 
     lax.fori_loop(0, nn, fold, 0)
 
+    def to_core(w):
+        return pltpu.make_async_remote_copy(
+            src_ref=terms.at[1 - my_core, w],
+            dst_ref=from_core.at[w],
+            send_sem=core_send.at[w],
+            recv_sem=core_recv.at[w],
+            device_id=(my_w, my_z * 2 + 1 - my_core),
+            device_id_type=MESH,
+        )
+
+    def to_wide(other, source):
+        return pltpu.make_async_remote_copy(
+            src_ref=terms.at[my_core, other],
+            dst_ref=from_wide.at[source],
+            send_sem=wide_send.at[other],
+            recv_sem=wide_recv.at[source],
+            device_id=(other, my_n),
+            device_id_type=MESH,
+        )
+
+    def to_z(other, source):
+        return pltpu.make_async_remote_copy(
+            src_ref=terms.at[my_core, my_w, other],
+            dst_ref=from_z.at[source],
+            send_sem=z_send.at[other],
+            recv_sem=z_recv.at[source],
+            device_id=(my_w, other * 2 + my_core),
+            device_id_type=MESH,
+        )
+
+    wides = [lax.rem(my_w + step, nw) for step in range(1, nw)]
+    levels = [lax.rem(my_z + step, zs) for step in range(1, zs)]
+    for w in wides + [my_w]:
+        to_core(w).start()
+    for w in wides + [my_w]:
+        to_core(w).wait_recv()
+        terms[my_core, w] = terms[my_core, w] + from_core[w]
+        if w is not my_w:
+            to_wide(w, my_w).start()
+    for w in wides:
+        to_wide(w, w).wait_recv()
+    for z in levels + [my_z]:
+        total = terms[my_core, my_w, z]
+        for w in wides:
+            total = total + from_wide[w, z]
+        terms[my_core, my_w, z] = total
+        if z is not my_z:
+            to_z(z, my_z).start()
+    total = terms[my_core, my_w, my_z]
+    for z in levels:
+        to_z(z, z).wait_recv()
+        total = total + from_z[z]
+    out_ref[...] = total
+
+    for step in range(1, nn):
+        orbital_copy(lax.rem(my_n + step, nn), my_n).wait_send()
+    for w in wides + [my_w]:
+        to_core(w).wait_send()
+    for w in wides:
+        to_wide(w, my_w).wait_send()
+    for z in levels:
+        to_z(z, my_z).wait_send()
     for chunk in range(chunks):
         def sent(step, carry, chunk=chunk):
             outgoing(chunk, lax.rem(me + step, ndev)).wait_send()
@@ -130,27 +227,42 @@
     ndev = nw * nn
     chunks = occ // (2 * ndev)
     lanes = 2 * ao_local
-    block = basis // pattern.shape[2]
-    keep = jnp.repeat(pattern[0, 0], block).astype(jnp.bfloat16)
-    ct = (lax.all_gather(orbitals, "narrow", axis=0, tiled=True) * keep[:, None]).T
-    term = pl.pallas_call(
+    rows = ao_local // nw
+    assert pattern.shape == (1, 1, nn) and basis == nn * ao_local and occ == chunks * 2 * ndev
+    vmem = pl.BlockSpec(memory_space=pltpu.VMEM)
+    return pl.pallas_call(
         functools.partial(kernel, nw, nn),
-        out_shape=jax.ShapeDtypeStruct((basis, basis), jnp.float32),
-        in_specs=[pl.BlockSpec(memory_space=pltpu.VMEM)] * 3,
-        out_specs=pl.BlockSpec(memory_space=pltpu.VMEM),
+        out_shape=jax.ShapeDtypeStruct((rows, basis), jnp.float32),
+        in_specs=[pl.BlockSpec(memory_space=pltpu.SMEM), pl.BlockSpec(memory_space=pl.ANY), vmem, vmem],
+        out_specs=vmem,
         scratch_shapes=[
+            pltpu.VMEM(tensor3.shape, jnp.bfloat16),
+            pltpu.VMEM((nn, ao_local, occ), jnp.bfloat16),
+            pltpu.VMEM((occ, basis), jnp.bfloat16),
             pltpu.VMEM((ri_local // 2 * occ, lanes), jnp.float32),
             pltpu.VMEM((chunks, ndev, ri_local, lanes), jnp.bfloat16),
             pltpu.VMEM((chunks, nw * ri_local, nn * lanes), jnp.bfloat16),
             pltpu.VMEM((nn * lanes, nn * lanes), jnp.float32),
+            pltpu.VMEM((2, nw, nn // 2, rows, basis), jnp.float32),
+            pltpu.VMEM((nw, nn // 2, rows, basis), jnp.float32),
+            pltpu.VMEM((nw, nn // 2, rows, basis), jnp.float32),
+            pltpu.VMEM((nn // 2, rows, basis), jnp.float32),
+            pltpu.SemaphoreType.DMA,
+            pltpu.SemaphoreType.DMA((nn,)),
+            pltpu.SemaphoreType.DMA((nn,)),
             pltpu.SemaphoreType.DMA((chunks,)),
             pltpu.SemaphoreType.DMA((chunks,)),
+            pltpu.SemaphoreType.DMA((nw,)),
+            pltpu.SemaphoreType.DMA((nw,)),
+            pltpu.SemaphoreType.DMA((nw,)),
+            pltpu.SemaphoreType.DMA((nw,)),
+            pltpu.SemaphoreType.DMA((nn // 2,)),
+            pltpu.SemaphoreType.DMA((nn // 2,)),
         ],
         compiler_params=pltpu.CompilerParams(
             collective_id=0, has_side_effects=True, vmem_limit_bytes=56 * 1024 * 1024
         ),
-    )(tensor3, ct, metric)
-    return lax.psum_scatter(term, ("wide", "narrow"), scatter_dimension=0, tiled=True)
+    )(pattern, tensor3, orbitals, metric)
 
 
 def solution(mesh):

time: 225 us -> 86.1 us (0.38)
  waiting for transfers between devices: 136 us -> 0 us
  Pallas kernels: 58.5 us -> 84.5 us
  blocking collectives: 16.1 us -> 0 us
  between operations: 13.4 us -> 0.01 us
    reduce_scatter x1 -> x0, waiting for transfers between devices: 136 us -> none  [body(): lax.psum_scatter(term, ('wide', 'narrow'), scatter_dimension=0, tiled=True)]
    pallas_call x1, Pallas kernels: 58.5 us -> 84.5 us  [body(): pl.pallas_call(functools.partial(kernel, nw, nn), out_shape=jax.ShapeDtyp...]
    all_gather x1 -> x0, blocking collectives: 16.1 us -> none  [body(): lax.all_gather(orbitals, 'narrow', axis=0, tiled=True) * keep[:, None]]
  transfers between devices with their start and end apart: 1 -> 0, of which waited for: 1 -> 0; matrix products, arithmetic and copies ran while one was open for 0% -> 0% of each run, Pallas kernels for 0% -> 0%
where the time goes in v2:
time: 86.1 us; the launch traced here: 85.9 us
  Pallas kernels  84.5 us (98%)
  local copies, waits for them, and re-layouts  1.38 us (2%)
    pallas_call x1, Pallas kernels, body(): pl.pallas_call(functools.partial(kernel, nw, nn), out_shape=jax.ShapeDtyp...  84.5 us

profile of v2, /device:TPU:0, one launch (start us, length us, event | category | flops | bytes accessed | tf_op | source)
XLA Modules:
  0.0 85.9 jit_solution(18304127779409224074)
XLA Ops:
  0.0 84.5 %shard_map.46 = f32[16,512]{1,0:T(8,128)} custom-call(s32[1,1,8]{2,1,0:T(1,128)} %pattern_ref.1, bf16[64,64,512]{2,1,0:T(8,128)(2,1)} %t_hbm.1, bf16[64,256]{1,0:T(8,128)(2,1)} %orb_ref.1, bf16[256,256]{1,0:T(8,128)(2,1)} %metric_ref.1), custom_call_target="tpu_custom_call" | custom-call | tf_op jit(solution)/shard_map/pallas_call | solution.py:233
  84.5 1.4 %copy.6 = f32[16,512]{1,0:T(8,128)} copy(f32[16,512]{1,0:T(8,128)} %shard_map.46) | data formatting | bytes 65536

commit v3 on v2

v3 whole, which is shorter than its diff:
```python
import functools

import jax
import jax.numpy as jnp
from jax import lax
from jax.experimental import pallas as pl
from jax.experimental.pallas import tpu as pltpu
from jax.sharding import PartitionSpec as P

MESH = pl.DeviceIdType.MESH


def kernel(nw, nn, pattern_ref, t_hbm, orb_ref, metric_ref, out_ref, t_ref, orbs, ct_ref, wide_c, send, recv, gram,
           terms, from_core, from_wide, from_z, t_sem, orb_send, orb_recv, pass_send, send_sem, recv_sem,
           core_send, core_recv, wide_send, wide_recv, z_send, z_recv):
    ndev = nw * nn
    ri_local, ao_local, _ = t_ref.shape
    occ = ct_ref.shape[0]
    part = ri_local // 4
    lanes = 2 * ao_local
    chunks = occ // (2 * ndev)
    zs = nn // 2
    my_w, my_n = lax.axis_index("wide"), lax.axis_index("narrow")
    me = my_w * nn + my_n
    my_z, my_core = my_n // 2, lax.rem(my_n, 2)

    t_copy = pltpu.make_async_copy(t_hbm, t_ref, t_sem)
    t_copy.start()
    barrier = pltpu.get_barrier_semaphore()

    def greet(step, carry):
        other = lax.rem(me + step, ndev)
        pl.semaphore_signal(
            barrier, inc=1, device_id=(other // nn, lax.rem(other, nn)), device_id_type=MESH
        )
        return carry

    lax.fori_loop(1, ndev, greet, 0)
    pl.semaphore_wait(barrier, ndev - 1)

    levels = [lax.rem(my_z + step, zs) for step in range(1, zs)]

    def orbital_copy(z, core, source):
        return pltpu.make_async_remote_copy(
            src_ref=orb_ref,
            dst_ref=orbs.at[source],
            send_sem=orb_send.at[z * 2 + core],
            recv_sem=orb_recv.at[source],
            device_id=(my_w, z * 2 + core),
            device_id_type=MESH,
        )

    def forward(z):
        return pltpu.make_async_remote_copy(
            src_ref=orbs.at[z * 2 + my_core],
            dst_ref=orbs.at[z * 2 + my_core],
            send_sem=pass_send.at[z],
            recv_sem=orb_recv.at[z * 2 + my_core],
            device_id=(my_w, my_z * 2 + 1 - my_core),
            device_id_type=MESH,
        )

    def landed(source):
        pltpu.make_async_remote_copy(
            src_ref=orb_ref, dst_ref=orbs.at[source], send_sem=orb_send.at[source],
            recv_sem=orb_recv.at[source], device_id=(my_w, source), device_id_type=MESH,
        ).wait_recv()

    for z in levels:
        orbital_copy(z, my_core, my_n).start()
    orbital_copy(my_z, 1 - my_core, my_n).start()
    orbs[my_n] = orb_ref[...]
    for z in levels:
        landed(z * 2 + my_core)
        forward(z).start()
    for z in [my_z] + levels:
        landed(z * 2 + 1 - my_core)
        kept = [
            orbs[n].astype(jnp.float32) * pattern_ref[0, 0, n].astype(jnp.float32)
            for n in (2 * z, 2 * z + 1)
        ]
        at = pl.ds(pl.multiple_of(z * lanes, lanes), lanes)
        ct_ref[:, at] = jnp.concatenate(kept, axis=0).T.astype(jnp.bfloat16)
    t_copy.wait()

    def contract(step, carry):
        r = step * 2
        first = r // part * 2 * part + lax.rem(r, part)
        rows = jnp.concatenate(
            [t_ref[first], t_ref[first + part], t_ref[first + 1], t_ref[first + part + 1]], axis=0
        )
        out = lax.dot_general(
            ct_ref[...], rows, (((1,), (1,)), ((), ())), preferred_element_type=jnp.float32
        )
        start = pl.multiple_of(r * occ, 2 * occ)
        wide_c[pl.ds(start, occ), :] = out[:, :lanes]
        wide_c[pl.ds(start + occ, occ), :] = out[:, lanes:]
        return carry

    low = lax.broadcasted_iota(jnp.int32, (part, lanes), 1) < ao_local
    lanes_here = pl.ds(pl.multiple_of(my_n * lanes, lanes), lanes)

    def pack(chunk, other, group):
        at = group * part * occ + chunk * 2 * ndev + other
        first = wide_c[pl.ds(at, part, stride=occ), :]
        second = wide_c[pl.ds(at + ndev, part, stride=occ), :]
        top = jnp.where(low, first, pltpu.roll(second, ao_local, 1))
        bottom = jnp.where(low, pltpu.roll(first, ao_local, 1), second)
        send[chunk, other, pl.ds(group * 2 * part, 2 * part)] = jnp.concatenate(
            [top, bottom], axis=0
        ).astype(jnp.bfloat16)

    def rows_here(start, count):
        return pl.ds(pl.multiple_of(my_w * ri_local + start, count), count)

    def outgoing(chunk, other, start, count):
        return pltpu.make_async_remote_copy(
            src_ref=send.at[chunk, other, pl.ds(start, count)],
            dst_ref=recv.at[chunk, rows_here(start, count), lanes_here],
            send_sem=send_sem.at[chunk],
            recv_sem=recv_sem.at[chunk],
            device_id=(other // nn, lax.rem(other, nn)),
            device_id_type=MESH,
        )

    def to_all(act):
        far = [zs // 2] + [x for x in range(1, zs) if x != zs // 2] + [0]
        for x in far:
            def one(step, carry, x=x):
                w = lax.rem(my_w + step // 2, nw)
                core = lax.rem(my_core + step, 2)
                act(w * nn + lax.rem(my_z + x, zs) * 2 + core)
                return carry

            lax.fori_loop(0 if x else 1, 2 * nw, one, 0)

    for group in range(2):
        lax.fori_loop(group * part // 2, (group + 1) * part // 2, contract, 0)

        def ship_part(other, group=group):
            pack(0, other, group)
            outgoing(0, other, group * 2 * part, 2 * part).start()

        to_all(ship_part)
        pack(0, me, group)
    for chunk in range(1, chunks):
        def ship(other, chunk=chunk):
            pack(chunk, other, 0)
            pack(chunk, other, 1)
            outgoing(chunk, other, 0, ri_local).start()

        to_all(ship)
        pack(chunk, me, 0)
        pack(chunk, me, 1)
    for chunk in range(chunks):
        pltpu.make_async_copy(
            send.at[chunk, me], recv.at[chunk, rows_here(0, ri_local), lanes_here], recv_sem.at[chunk]
        ).start()

    per = nn // nw
    width = per * lanes

    def arrived(chunk):
        pltpu.make_async_copy(recv.at[chunk], recv.at[chunk], recv_sem.at[chunk]).wait()

    def fit(chunk, w):
        at = pl.ds(pl.multiple_of(w * width, width), width)
        fitted = jnp.dot(
            metric_ref[...], recv[chunk, :, at], preferred_element_type=jnp.float32
        ).astype(jnp.bfloat16)
        term = lax.dot_general(
            fitted, recv[chunk], (((0,), (0,)), ((), ())), preferred_element_type=jnp.float32
        )
        gram[at, :] = term if chunk == 0 else gram[at, :] + term

    for chunk in range(chunks - 1):
        arrived(chunk)

        def fit_one(w, carry, chunk=chunk):
            fit(chunk, w)
            return carry

        lax.fori_loop(0, nw, fit_one, 0)

    left = lax.broadcasted_iota(jnp.int32, (ao_local, lanes), 1) < ao_local
    rows = ao_local // nw

    def fold(w):
        for n in range(per):
            start = w * width + n * lanes
            even = pl.ds(pl.multiple_of(start, lanes), ao_local)
            odd = pl.ds(pl.multiple_of(start + ao_local, ao_local), ao_local)
            for pair in range(nn // 2):
                one, two = pl.ds(2 * pair * lanes, lanes), pl.ds((2 * pair + 1) * lanes, lanes)
                here = jnp.where(left, gram[even, one], gram[odd, two])
                there = jnp.where(left, gram[even, two], gram[odd, one])
                folded = -(here + pltpu.roll(there, ao_local, 1))
                for q in range(nw):
                    terms[q % 2, w, (n * nw + q) // 2, :, pl.ds(pair * lanes, lanes)] = (
                        folded[q * rows:(q + 1) * rows]
                    )

    def to_core(w):
        return pltpu.make_async_remote_copy(
            src_ref=terms.at[1 - my_core, w],
            dst_ref=from_core.at[w],
            send_sem=core_send.at[w],
            recv_sem=core_recv.at[w],
            device_id=(my_w, my_z * 2 + 1 - my_core),
            device_id_type=MESH,
        )

    def to_wide(other, source):
        return pltpu.make_async_remote_copy(
            src_ref=terms.at[my_core, other],
            dst_ref=from_wide.at[source],
            send_sem=wide_send.at[other],
            recv_sem=wide_recv.at[source],
            device_id=(other, my_n),
            device_id_type=MESH,
        )

    def to_z(other, source):
        return pltpu.make_async_remote_copy(
            src_ref=terms.at[my_core, my_w, other],
            dst_ref=from_z.at[source],
            send_sem=z_send.at[other],
            recv_sem=z_recv.at[source],
            device_id=(my_w, other * 2 + my_core),
            device_id_type=MESH,
        )

    wides = [lax.rem(my_w + step, nw) for step in range(1, nw)]
    def pass_on(w):
        to_core(w).wait_recv()
        terms[my_core, w] = terms[my_core, w] + from_core[w]
        if w is not my_w:
            to_wide(w, my_w).start()

    arrived(chunks - 1)
    before = None
    for w in wides + [my_w]:
        fit(chunks - 1, w)
        fold(w)
        to_core(w).start()
        if before is not None:
            pass_on(before)
        before = w
    pass_on(before)
    for w in wides:
        to_wide(w, w).wait_recv()
    for z in levels + [my_z]:
        total = terms[my_core, my_w, z]
        for w in wides:
            total = total + from_wide[w, z]
        terms[my_core, my_w, z] = total
        if z is not my_z:
            to_z(z, my_z).start()
    total = terms[my_core, my_w, my_z]
    for z in levels:
        to_z(z, z).wait_recv()
        total = total + from_z[z]
    out_ref[...] = total

    for z in levels:
        orbital_copy(z, my_core, my_n).wait_send()
        forward(z).wait_send()
    orbital_copy(my_z, 1 - my_core, my_n).wait_send()
    for w in wides + [my_w]:
        to_core(w).wait_send()
    for w in wides:
        to_wide(w, my_w).wait_send()
    for z in levels:
        to_z(z, my_z).wait_send()
    for chunk in range(chunks):
        def sent(other, chunk=chunk):
            outgoing(chunk, other, 0, ri_local).wait_send()

        to_all(sent)


def body(nw, nn, tensor3, pattern, orbitals, metric):
    ri_local, ao_local, basis = tensor3.shape
    occ = orbitals.shape[1]
    ndev = nw * nn
    chunks = occ // (2 * ndev)
    lanes = 2 * ao_local
    rows = ao_local // nw
    assert pattern.shape == (1, 1, nn) and basis == nn * ao_local and occ == chunks * 2 * ndev
    vmem = pl.BlockSpec(memory_space=pltpu.VMEM)
    return pl.pallas_call(
        functools.partial(kernel, nw, nn),
        out_shape=jax.ShapeDtypeStruct((rows, basis), jnp.float32),
        in_specs=[pl.BlockSpec(memory_space=pltpu.SMEM), pl.BlockSpec(memory_space=pl.ANY), vmem, vmem],
        out_specs=vmem,
        scratch_shapes=[
            pltpu.VMEM(tensor3.shape, jnp.bfloat16),
            pltpu.VMEM((nn, ao_local, occ), jnp.bfloat16),
            pltpu.VMEM((occ, basis), jnp.bfloat16),
            pltpu.VMEM((ri_local // 2 * occ, lanes), jnp.float32),
            pltpu.VMEM((chunks, ndev, ri_local, lanes), jnp.bfloat16),
            pltpu.VMEM((chunks, nw * ri_local, nn * lanes), jnp.bfloat16),
            pltpu.VMEM((nn * lanes, nn * lanes), jnp.float32),
            pltpu.VMEM((2, nw, nn // 2, rows, basis), jnp.float32),
            pltpu.VMEM((nw, nn // 2, rows, basis), jnp.float32),
            pltpu.VMEM((nw, nn // 2, rows, basis), jnp.float32),
            pltpu.VMEM((nn // 2, rows, basis), jnp.float32),
            pltpu.SemaphoreType.DMA,
            pltpu.SemaphoreType.DMA((nn,)),
            pltpu.SemaphoreType.DMA((nn,)),
            pltpu.SemaphoreType.DMA((nn // 2,)),
            pltpu.SemaphoreType.DMA((chunks,)),
            pltpu.SemaphoreType.DMA((chunks,)),
            pltpu.SemaphoreType.DMA((nw,)),
            pltpu.SemaphoreType.DMA((nw,)),
            pltpu.SemaphoreType.DMA((nw,)),
            pltpu.SemaphoreType.DMA((nw,)),
            pltpu.SemaphoreType.DMA((nn // 2,)),
            pltpu.SemaphoreType.DMA((nn // 2,)),
        ],
        compiler_params=pltpu.CompilerParams(
            collective_id=0, has_side_effects=True, vmem_limit_bytes=56 * 1024 * 1024
        ),
    )(pattern, tensor3, orbitals, metric)


def solution(mesh):
    nw, nn = mesh.shape["wide"], mesh.shape["narrow"]
    in_specs = (P("wide", "narrow", None), P("wide", "narrow", None), P("narrow", None), P())
    out_specs = P(("wide", "narrow"), None)
    return jax.shard_map(
        functools.partial(body, nw, nn), mesh=mesh, in_specs=in_specs, out_specs=out_specs, check_vma=False
    )
```

time: 86.1 us -> 79.6 us (0.925)
  Pallas kernels: 84.5 us -> 78 us
    pallas_call x1, Pallas kernels: 84.5 us -> 78 us  [body(): pl.pallas_call(functools.partial(kernel, nw, nn), out_shape=jax.ShapeDtyp...]
where the time goes in v3:
time: 79.6 us; the launch traced here: 79.4 us
  Pallas kernels  78 us (98%)
  local copies, waits for them, and re-layouts  1.38 us (2%)
    pallas_call x1, Pallas kernels, body(): pl.pallas_call(functools.partial(kernel, nw, nn), out_shape=jax.ShapeDtyp...  78 us

profile of v3, /device:TPU:0, one launch (start us, length us, event | category | flops | bytes accessed | tf_op | source)
XLA Modules:
  0.0 79.4 jit_solution(15506986463302029427)
XLA Ops:
  0.0 78.0 %shard_map.46 = f32[16,512]{1,0:T(8,128)} custom-call(s32[1,1,8]{2,1,0:T(1,128)} %pattern_ref.1, bf16[64,64,512]{2,1,0:T(8,128)(2,1)} %t_hbm.1, bf16[64,256]{1,0:T(8,128)(2,1)} %orb_ref.1, bf16[256,256]{1,0:T(8,128)(2,1)} %metric_ref.1), custom_call_target="tpu_custom_call" | custom-call | tf_op jit(solution)/shard_map/pallas_call | solution.py:291
  78.0 1.4 %copy.6 = f32[16,512]{1,0:T(8,128)} copy(f32[16,512]{1,0:T(8,128)} %shard_map.46) | data formatting | bytes 65536
